TPU v7x, 32 devices: a whole 2x2x4 slice. The times are simulated.
32 devices in a mesh: groups: 2 (over y), gx: 8 (over z, x), gy: 2 (over core).
Axes of the slice: x: 2, y: 2, z: 4, core: 2. Of those that a mesh axis runs over, the one named last changes fastest.
Arguments:
- tokens: bfloat16 [512, 6144], P('groups', ('gy', 'gx')), parts along dimension 0, may hold values from -6 to 6
- ln_gain: bfloat16 [6144], P('gy'), may hold values from 0.099609375 to 1.8984375
- up_weight: bfloat16 [6144, 24576], P('gy', 'gx'), may hold values from -0.078125 to 0.078125
- up_bias: bfloat16 [24576], P('gx'), may hold values from -4 to 4
- down_weight: bfloat16 [24576, 6144], P('gx', 'gy'), may hold values from -0.0546875 to 0.0546875
- down_bias: bfloat16 [6144], P(('gy', 'gx')), may hold values from -3 to 3
Outputs:
- layer_out: bfloat16 [512, 6144], P('groups', ('gy', 'gx')), parts along dimension 0
There are 2 independent parts, one for each index of `groups`. A program takes and returns all parts, laid end to end along the dimension named above; an argument that names none is the same for every part. Nothing has to cross between parts.
All inputs are finite; a program needn't handle non-finite values.
Results may differ from a plain program's by a relative error of at most 0.0049.
Values may be sent and summed in bfloat16 or wider, within the bound.
A program may use at most 128 MiB of HBM per device.

v0:
```python
import jax
import jax.numpy as jnp
from jax import lax
from jax.sharding import PartitionSpec as P


def normalize(values, first, second, width, gain_part):
    mean = (first / width)[:, None]
    square = (second / width)[:, None]
    scale = lax.rsqrt(square - mean * mean + 1e-06)
    return ((values - mean) * scale * gain_part.astype(jnp.float32)).astype(jnp.bfloat16)


def shards(tokens, ln_gain, up_weight, up_bias, down_weight, down_bias):
    width = tokens.shape[1] * lax.axis_size("gy") * lax.axis_size("gx")
    values = tokens.astype(jnp.float32)
    gathered = lax.all_gather(tokens, "gx", axis=1, tiled=True)
    all_values = gathered.astype(jnp.float32)
    first, second = lax.psum(
        (jnp.sum(all_values, axis=-1), jnp.sum(all_values * all_values, axis=-1)), "gy"
    )
    normed = normalize(all_values, first, second, width, ln_gain)
    partial_value = jnp.dot(normed, up_weight, preferred_element_type=jnp.float32)
    bias_up = up_bias.astype(jnp.float32)
    share = lax.psum_scatter(partial_value, "gy", scatter_dimension=0, tiled=True)
    hidden = jax.nn.gelu(share + bias_up, approximate=False).astype(jnp.bfloat16)
    terms = jnp.dot(
        lax.all_gather(hidden, "gy", axis=0, tiled=True),
        down_weight,
        preferred_element_type=jnp.float32,
    )
    branch = lax.psum_scatter(terms, "gx", scatter_dimension=1, tiled=True)
    return (values + branch + down_bias.astype(jnp.float32)).astype(jnp.bfloat16)


def solution(mesh):
    in_specs = (
        P("groups", ("gy", "gx")),
        P("gy"),
        P("gy", "gx"),
        P("gx"),
        P("gx", "gy"),
        P(("gy", "gx")),
    )
    out_specs = P("groups", ("gy", "gx"))
    return jax.shard_map(shards, mesh=mesh, in_specs=in_specs, out_specs=out_specs, check_vma=False)
```

profile of v0, /device:TPU:0, one launch (start us, length us, event | category | flops | bytes accessed | tf_op | source)
XLA Modules:
  0.0 193.2 jit_solution(10235211324114134998)
XLA Ops:
  6.5 0.0 all-gather.3.cloned.1.call-start
  6.5 0.7 all-gather.3.cloned.1.call-update
  7.3 0.0 reduce-scatter.3.cloned.1.call-start
  7.3 0.7 convert_element_type.26
  8.0 49.5 %all-gather.3.cloned.1.call-done = bf16[256,3072]{1,0:T(8,128)(2,1)} async-done(((bf16[256,384]{1,0:T(8,128)(2,1)}), bf16[256,3072]{1,0:T(8,128)(2,1)}) %all-gather.3.cloned.1.call-update) | async-done | bytes 1572880 | tf_op jit(solution)/shard_map/all_gather | solution.py:17
  57.5 0.0 copy-start
  57.5 2.1 %convert_reduce_fusion = (f32[256]{0:T(256)S(1)}, f32[256]{0:T(256)S(1)}) fusion(bf16[256,3072]{1,0:T(8,128)(2,1)} %all-gather.3.cloned.1.call-done), kind=kLoop, calls=%fused_computation.2 | loop fusion | flops 3145216 | bytes 1574912 | tf_op jit(solution)/shard_map/reduce_sum | solution.py:20
  59.6 2.5 %all-reduce = (f32[256]{0:T(256)S(1)}, f32[256]{0:T(256)S(1)}) all-reduce(f32[256]{0:T(256)S(1)} %get-tuple-element.6, f32[256]{0:T(256)S(1)} %get-tuple-element.5), channel_id=1, replica_groups=mesh['groups'=2,'gx'=8,'gy'=2] {'gy'}, use_global_device_ids=true, to_apply=%region_3.0 | all-reduce | flops 512 | bytes 4096 | tf_op jit(solution)/shard_map/psum | solution.py:19
  62.1 0.0 copy-done
  62.1 10.9 %fusion.7 = f32[256,3072]{1,0:T(8,128)} fusion(bf16[3072,3072]{1,0:T(8,128)(2,1)} %param.8, bf16[256,3072]{1,0:T(8,128)(2,1)S(1)} %copy-done, f32[3072]{0:T(1024)S(1)} %convert_element_type.26, f32[256]{0:T(256)S(1)} %get-tuple-element.10, f32[256]{0:T(256)S(1)} %get-tuple-element.9), kind=kOutput, calls=%fused_computation.11 | convolution fusion | flops 4835770368 | bytes 23607296 | tf_op jit(solution)/shard_map/dot_general | solution.py:23
  72.9 0.0 copy-start.2
  72.9 0.0 reduce-scatter.3.cloned.1.call-update
  73.0 0.0 all-gather.5.cloned.1.call-start
  73.0 0.6 copy-done.2
  73.6 8.6 %reduce-scatter.3.cloned.1.call-done = f32[128,3072]{1,0:T(8,128)} async-done(((f32[256,3072]{1,0:T(8,128)}), f32[128,3072]{1,0:T(8,128)}) %reduce-scatter.3.cloned.1.call-update) | async-done | bytes 1572880 | tf_op jit(solution)/shard_map/reduce_scatter | solution.py:25
  82.2 5.3 %fusion.6 = bf16[128,3072]{1,0:T(8,128)(2,1)} fusion(f32[128,3072]{1,0:T(8,128)} %reduce-scatter.3.cloned.1.call-done, f32[3072]{0:T(1024)S(1)} %convert_element_type.28), kind=kLoop, calls=%fused_computation.10 | loop fusion | flops 25952256 | bytes 2371584 | tf_op jit(solution)/shard_map/convert_element_type | solution.py:26
  87.5 0.0 all-gather.5.cloned.1.call-update
  87.6 0.0 reduce-scatter.5.cloned.1.call-start
  87.6 11.1 %all-gather.5.cloned.1.call-done = bf16[256,3072]{1,0:T(8,128)(2,1)} async-done(((bf16[128,3072]{1,0:T(8,128)(2,1)}), bf16[256,3072]{1,0:T(8,128)(2,1)}) %all-gather.5.cloned.1.call-update) | async-done | bytes 1572880 | tf_op jit(solution)/shard_map/all_gather | solution.py:28
  98.7 10.6 %fusion.19 = f32[256,3072]{1,0:T(8,128)} fusion(bf16[256,3072]{1,0:T(8,128)(2,1)} %all-gather.5.cloned.1.call-done, bf16[3072,3072]{1,0:T(8,128)(2,1)} %param.10), kind=kOutput, calls=%fused_computation.33 | convolution fusion | flops 4831838208 | bytes 23592960 | tf_op jit(solution)/shard_map/dot_general | solution.py:27
  109.2 0.0 copy-start.3
  109.2 0.0 copy-start.1
  109.2 0.0 reduce-scatter.5.cloned.1.call-update
  109.3 0.7 copy-done.3
  109.9 75.0 %reduce-scatter.5.cloned.1.call-done = f32[256,384]{1,0:T(8,128)} async-done(((f32[256,3072]{1,0:T(8,128)}), f32[256,384]{1,0:T(8,128)}) %reduce-scatter.5.cloned.1.call-update) | async-done | bytes 393232 | tf_op jit(solution)/shard_map/reduce_scatter | solution.py:32
  184.9 0.0 copy-done.1
  184.9 1.7 add_convert_fusion
  (3 shorter events, 0.0 us)
Async XLA Ops:
  6.5 50.9 %all-gather.3.cloned.1.call-start = ((), (), s32[]{:S(2)}) async-start(), calls=%async_computation.2 | async-start | bytes 1769472 | tf_op jit(solution)/shard_map/all_gather | solution.py:17
  7.3 75.0 %reduce-scatter.3.cloned.1.call-start = ((), (), s32[]{:S(2)}) async-start(), calls=%async_computation.3 | async-start | bytes 4718592 | tf_op jit(solution)/shard_map/reduce_scatter | solution.py:25
  57.5 4.6 %copy-start = (bf16[256,3072]{1,0:T(8,128)(2,1)S(1)}, bf16[256,3072]{1,0:T(8,128)(2,1)}, u32[]{:S(2)}) copy-start(bf16[256,3072]{1,0:T(8,128)(2,1)} %all-gather.3.cloned.1.call-done) | copy-start | bytes 4718596
  72.9 0.7 copy-start.2
  73.0 25.7 %all-gather.5.cloned.1.call-start = ((), (), s32[]{:S(2)}) async-start(), calls=%async_computation.4 | async-start | bytes 2359296 | tf_op jit(solution)/shard_map/all_gather | solution.py:28
  87.6 97.3 %reduce-scatter.5.cloned.1.call-start = ((), (), s32[]{:S(2)}) async-start(), calls=%async_computation.5 | async-start | bytes 3538944 | tf_op jit(solution)/shard_map/reduce_scatter | solution.py:32
  109.2 0.7 copy-start.3
  109.2 75.7 %copy-start.1 = (bf16[256,384]{1,0:T(8,128)(2,1)S(1)}, bf16[256,384]{1,0:T(8,128)(2,1)}, u32[]{:S(2)}) copy-start(bf16[256,384]{1,0:T(8,128)(2,1)} %param.6) | copy-start | bytes 589828
Sparse Core Ops, SparseCore 0:
  9.4 47.9 all-gather.2
  73.1 9.0 reduce-scatter.2
  87.7 10.9 all-gather.4
  109.4 75.4 reduce-scatter.4
where the time goes:
time: 193 us
  waiting for transfers between devices  145 us (75%)
  matrix products  21.4 us (11%)
  between operations  13.1 us (7%)
  other arithmetic  9.9 us (5%)
  blocking collectives  2.47 us (1%)
    reduce_scatter x1, waiting for transfers between devices, shards(): branch = lax.psum_scatter(terms, 'gx', scatter_dimension=1, tiled=True)  75 us
    all_gather x1, waiting for transfers between devices, shards(): gathered = lax.all_gather(tokens, 'gx', axis=1, tiled=True)  49.5 us
    all_gather x1, waiting for transfers between devices, shards(): lax.all_gather(hidden, 'gy', axis=0, tiled=True)  11.1 us
    dot_general x1, matrix products, shards(): jnp.dot(normed, up_weight, preferred_element_type=jnp.float32)  10.9 us
    dot_general x1, matrix products, shards(): jnp.dot(lax.all_gather(hidden, 'gy', axis=0, tiled=True), down_weight, pr...  10.6 us
    reduce_scatter x1, waiting for transfers between devices, shards(): lax.psum_scatter(partial_value, 'gy', scatter_dimension=0, tiled=True)  8.59 us
    convert_element_type x1, other arithmetic, shards(): jax.nn.gelu(share + bias_up, approximate=False).astype(jnp.bfloat16)  5.33 us
  transfers between devices with their start and end apart: 4, of which 4 were waited for; matrix products, arithmetic and copies ran while one was open for 0% of the time, Pallas kernels for 0%

commit v1 on v0

--- a/solution.py
+++ b/solution.py
@@ -1,7 +1,18 @@
+import functools
+
 import jax
 import jax.numpy as jnp
 from jax import lax
+from jax.experimental import pallas as pl
+from jax.experimental.pallas import tpu as pltpu
 from jax.sharding import PartitionSpec as P
+
+MESH = pl.DeviceIdType.MESH
+F32 = jnp.float32
+BF16 = jnp.bfloat16
+LINES = 4
+CHUNKS = 2
+LANES = 128
 
 
 def normalize(values, first, second, width, gain_part):
@@ -33,6 +44,300 @@
     return (values + branch + down_bias.astype(jnp.float32)).astype(jnp.bfloat16)
 
 
+def kernel(
+    tok, gain, up_bias, down_bias, wu_hbm, wd_hbm, out,
+    wu, wd, line, cross, stat, mean_s, scale_s, nrm, acc, p_out, p_in, h_own, h_other,
+    y, x_out, x_in, z_out, z_in,
+    wu_sem, wd_sem, st_send, st_recv, az_send, az_recv, ax_send, ax_recv,
+    p_sem, h_sem, rx_send, rx_recv, rz_send, rz_recv,
+):
+    gx, gy = lax.axis_index("gx"), lax.axis_index("gy")
+    z, x = gx // 2, gx % 2
+    xo, go = 1 - x, 1 - gy
+    zs = (z, z + 1 - 2 * (z % 2), (z + 2) % LINES, LINES - 1 - z)
+    rows_all, wide = tok.shape
+    R = rows_all // CHUNKS
+    half = acc.shape[1] // 2
+    width = 16 * wide
+    to_x = {"gx": z * 2 + xo, "gy": gy}
+    to_y = {"gx": gx, "gy": go}
+    to_z = [{"gx": zs[j] * 2 + x, "gy": gy} for j in range(LINES)]
+
+    def rows(c):
+        return pl.ds(c * R, R)
+
+    def wu_copy(j, a, b):
+        src_row = (zs[j] * 2 + (x if a == 0 else xo)) * wide
+        src_col = (gy if b == 0 else go) * half
+        return pltpu.make_async_copy(
+            wu_hbm.at[pl.ds(pl.multiple_of(src_row, wide), wide), pl.ds(pl.multiple_of(src_col, half), half)],
+            wu.at[j, pl.ds(a * wide, wide), pl.ds(b * half, half)],
+            wu_sem.at[j, a, b],
+        )
+
+    def wd_copy(j, a, b):
+        src_row = (gy if a == 0 else go) * half
+        src_col = (zs[j] * 2 + (x if b == 0 else xo)) * wide
+        return pltpu.make_async_copy(
+            wd_hbm.at[pl.ds(pl.multiple_of(src_row, half), half), pl.ds(pl.multiple_of(src_col, wide), wide)],
+            wd.at[j, pl.ds(a * half, half), pl.ds(b * wide, wide)],
+            wd_sem.at[j, a, b],
+        )
+
+    four = [(a, b) for a in range(2) for b in range(2)]
+    for j in range(LINES):
+        for a, b in four:
+            wu_copy(j, a, b).start()
+    for j in reversed(range(LINES)):
+        for a, b in four:
+            wd_copy(j, a, b).start()
+
+    me = gx * 2 + gy
+    peers = [(me + d) % 16 for d in range(1, 16)]
+    barrier = pltpu.get_barrier_semaphore()
+    for p in peers:
+        pl.semaphore_signal(barrier, inc=1, device_id={"gx": p // 2, "gy": p % 2}, device_id_type=MESH)
+    pl.semaphore_wait(barrier, 15)
+
+    def remote(src, dst, send, recv, where):
+        return pltpu.make_async_remote_copy(
+            src_ref=src, dst_ref=dst, send_sem=send, recv_sem=recv, device_id=where, device_id_type=MESH
+        )
+
+    def gather_z(c, j):
+        return remote(tok.at[rows(c)], line.at[c, j], az_send.at[c, j], az_recv.at[c, j], to_z[j])
+
+    def gather_x(c, j):
+        src = tok.at[rows(c)] if j == 0 else line.at[c, j]
+        return remote(src, cross.at[c, j], ax_send.at[c, j], ax_recv.at[c, j], to_x)
+
+    def pre_copy(c):
+        return remote(p_out.at[c], p_in.at[c], p_sem.at[c, 0], p_sem.at[c, 1], to_y)
+
+    def hid_copy(c):
+        return remote(h_own.at[c], h_other.at[c], h_sem.at[c, 0], h_sem.at[c, 1], to_y)
+
+    def red_x(c, j):
+        return remote(x_out.at[c, j], x_in.at[c, j], rx_send.at[c, j], rx_recv.at[c, j], to_x)
+
+    def red_z(c, j):
+        return remote(z_out.at[c, j], z_in.at[c, j], rz_send.at[c, j], rz_recv.at[c, j], to_z[j])
+
+    def stat_copy(p):
+        return remote(stat.at[me], stat.at[me], st_send.at[p], st_recv.at[me], {"gx": p // 2, "gy": p % 2})
+
+    def stat_arrival(p):
+        return remote(stat.at[p], stat.at[p], st_send.at[p], st_recv.at[p], {"gx": p // 2, "gy": p % 2})
+
+    gather_x(0, 0).start()
+    for j in range(1, LINES):
+        gather_z(0, j).start()
+
+    v = tok[...].astype(F32)
+    first = jnp.sum(v, axis=1, keepdims=True)
+    second = jnp.sum(v * v, axis=1, keepdims=True)
+    lane = lax.broadcasted_iota(jnp.int32, (rows_all, LANES), 1)
+    both = jnp.where(lane == 0, first, jnp.where(lane == 1, second, 0.0))
+    stat[me] = both.T[0:8, :]
+    for p in peers:
+        stat_copy(p).start()
+    for p in peers:
+        stat_arrival(p).wait_recv()
+    total = stat[0]
+    for i in range(1, 16):
+        total = total + stat[i]
+    full = jnp.concatenate([total, jnp.zeros((LANES - 8, rows_all), F32)], axis=0).T
+    mean = full[:, 0:1] / width
+    square = full[:, 1:2] / width
+    scale = lax.rsqrt(square - mean * mean + 1e-06)
+    mean_s[...] = jnp.broadcast_to(mean, (rows_all, LANES))
+    scale_s[...] = jnp.broadcast_to(scale, (rows_all, LANES))
+
+    def norm_into(c, j, a, src):
+        col = pl.multiple_of((zs[j] * 2 + (x if a == 0 else xo)) * wide, wide)
+        g = gain[:, pl.ds(col, wide)].astype(F32)
+        m = jnp.concatenate([mean_s[rows(c), :]] * (wide // LANES), axis=1)
+        s = jnp.concatenate([scale_s[rows(c), :]] * (wide // LANES), axis=1)
+        nrm[:, a * wide:(a + 1) * wide] = ((src.astype(F32) - m) * s * g).astype(BF16)
+
+    tile = 2 * wide
+    tiles = half // tile
+
+    def forward(c, j):
+        gather_z(c, j).wait_recv()
+        gather_x(c, j).start()
+
+    def up_step(c, j):
+        gather_x(c, j).wait_recv()
+        norm_into(c, j, 0, tok[rows(c), :] if j == 0 else line[c, j])
+        norm_into(c, j, 1, cross[c, j])
+        if c == 0:
+            for a, b in four:
+                wu_copy(j, a, b).wait()
+
+        def body(t, last):
+            cols = pl.ds(pl.multiple_of(t * tile, tile), tile)
+            part = jnp.dot(nrm[...], wu[j, :, cols], preferred_element_type=F32)
+            if j > 0:
+                part = part + acc[:, cols]
+            if last:
+                out_cols = pl.ds(pl.multiple_of((t - tiles) * tile, tile), tile)
+                p_out[c, :, out_cols] = part.astype(BF16)
+            else:
+                acc[:, cols] = part
+
+        if j == LINES - 1:
+            pl.loop(tiles, 2 * tiles)(lambda t: body(t, True))
+            pre_copy(c).start()
+            pl.loop(0, tiles)(lambda t: body(t, False))
+        else:
+            pl.loop(0, 2 * tiles)(lambda t: body(t, False))
+
+    def activate(c):
+        pre_copy(c).wait_recv()
+        step = 4 * LANES
+
+        @pl.loop(0, half // step)
+        def _(t):
+            cols = pl.ds(pl.multiple_of(t * step, step), step)
+            bias_cols = pl.ds(pl.multiple_of(gy * half + t * step, step), step)
+            pre = acc[:, cols] + p_in[c, :, cols].astype(F32) + up_bias[:, bias_cols].astype(F32)
+            h_own[c, :, cols] = (0.5 * pre * (1.0 + lax.erf(pre * 0.7071067811865476))).astype(BF16)
+
+        hid_copy(c).start()
+
+    def down_step(c, j):
+        if c == 0:
+            for a, b in four:
+                wd_copy(j, a, b).wait()
+        part = jnp.dot(h_own[c], wd[j, 0:half, :], preferred_element_type=F32)
+        part = part + jnp.dot(h_other[c], wd[j, half:, :], preferred_element_type=F32)
+        x_out[c, j] = part[:, wide:].astype(BF16)
+        red_x(c, j).start()
+        y[c, j] = part[:, :wide]
+
+    def pair_step(c, j):
+        red_x(c, j).wait_recv()
+        both = y[c, j] + x_in[c, j].astype(F32)
+        if j == 0:
+            y[c, j] = both
+        else:
+            z_out[c, j] = both.astype(BF16)
+            red_z(c, j).start()
+
+    def finish(c):
+        res = y[c, 0]
+        for j in range(1, LINES):
+            red_z(c, j).wait_recv()
+            res = res + z_in[c, j].astype(F32)
+        res = tok[rows(c), :].astype(F32) + res + down_bias[...].astype(F32)
+        out[rows(c), :] = res.astype(BF16)
+
+    forward(0, 1)
+    up_step(0, 0)
+    forward(0, 2)
+    up_step(0, 1)
+    forward(0, 3)
+    gather_x(1, 0).start()
+    for j in range(1, LINES):
+        gather_z(1, j).start()
+    up_step(0, 2)
+    up_step(0, 3)
+    forward(1, 1)
+    activate(0)
+    forward(1, 2)
+    up_step(1, 0)
+    hid_copy(0).wait_recv()
+    down_step(0, 3)
+    forward(1, 3)
+    down_step(0, 2)
+    up_step(1, 1)
+    down_step(0, 1)
+    down_step(0, 0)
+    up_step(1, 2)
+    pair_step(0, 3)
+    up_step(1, 3)
+    pair_step(0, 2)
+    activate(1)
+    pair_step(0, 1)
+    pair_step(0, 0)
+    hid_copy(1).wait_recv()
+    for j in reversed(range(LINES)):
+        down_step(1, j)
+    finish(0)
+    for j in reversed(range(LINES)):
+        pair_step(1, j)
+    finish(1)
+
+    for p in peers:
+        stat_copy(p).wait_send()
+    for c in range(CHUNKS):
+        pre_copy(c).wait_send()
+        hid_copy(c).wait_send()
+        for j in range(LINES):
+            gather_x(c, j).wait_send()
+            red_x(c, j).wait_send()
+            if j > 0:
+                gather_z(c, j).wait_send()
+                red_z(c, j).wait_send()
+
+
+def fused(tokens, ln_gain, up_weight, up_bias, down_weight, down_bias):
+    T, wide = tokens.shape
+    depth, hid = up_weight.shape
+    R, half = T // CHUNKS, hid // 2
+    vm = pl.BlockSpec(memory_space=pltpu.VMEM)
+    hbm = pl.BlockSpec(memory_space=pl.ANY)
+    dma = pltpu.SemaphoreType.DMA
+    scratch = [
+        pltpu.VMEM((LINES, 2 * wide, hid), BF16),
+        pltpu.VMEM((LINES, hid, 2 * wide), BF16),
+        pltpu.VMEM((CHUNKS, LINES, R, wide), BF16),
+        pltpu.VMEM((CHUNKS, LINES, R, wide), BF16),
+        pltpu.VMEM((16, 8, T), F32),
+        pltpu.VMEM((T, LANES), F32),
+        pltpu.VMEM((T, LANES), F32),
+        pltpu.VMEM((R, 2 * wide), BF16),
+        pltpu.VMEM((R, hid), F32),
+        pltpu.VMEM((CHUNKS, R, half), BF16),
+        pltpu.VMEM((CHUNKS, R, half), BF16),
+        pltpu.VMEM((CHUNKS, R, half), BF16),
+        pltpu.VMEM((CHUNKS, R, half), BF16),
+        pltpu.VMEM((CHUNKS, LINES, R, wide), F32),
+        pltpu.VMEM((CHUNKS, LINES, R, wide), BF16),
+        pltpu.VMEM((CHUNKS, LINES, R, wide), BF16),
+        pltpu.VMEM((CHUNKS, LINES, R, wide), BF16),
+        pltpu.VMEM((CHUNKS, LINES, R, wide), BF16),
+        dma((LINES, 2, 2)),
+        dma((LINES, 2, 2)),
+        dma((16,)),
+        dma((16,)),
+        dma((CHUNKS, LINES)),
+        dma((CHUNKS, LINES)),
+        dma((CHUNKS, LINES)),
+        dma((CHUNKS, LINES)),
+        dma((CHUNKS, 2)),
+        dma((CHUNKS, 2)),
+        dma((CHUNKS, LINES)),
+        dma((CHUNKS, LINES)),
+        dma((CHUNKS, LINES)),
+        dma((CHUNKS, LINES)),
+    ]
+    return pl.pallas_call(
+        kernel,
+        out_shape=jax.ShapeDtypeStruct((T, wide), BF16),
+        in_specs=[vm, vm, vm, vm, hbm, hbm],
+        out_specs=vm,
+        scratch_shapes=scratch,
+        compiler_params=pltpu.CompilerParams(
+            collective_id=0, has_side_effects=True, vmem_limit_bytes=60 * 1024 * 1024
+        ),
+        cost_estimate=pl.CostEstimate(
+            flops=4 * T * depth * hid, bytes_accessed=4 * depth * hid, transcendentals=T * half
+        ),
+    )(tokens, ln_gain.reshape(1, -1), up_bias.reshape(1, -1), down_bias.reshape(1, -1), up_weight, down_weight)
+
+
 def solution(mesh):
     in_specs = (
         P("groups", ("gy", "gx")),
@@ -43,4 +348,5 @@
         P(("gy", "gx")),
     )
     out_specs = P("groups", ("gy", "gx"))
-    return jax.shard_map(shards, mesh=mesh, in_specs=in_specs, out_specs=out_specs, check_vma=False)
+    body = fused if mesh.shape["gx"] == 2 * LINES and mesh.shape["gy"] == 2 else shards
+    return jax.shard_map(body, mesh=mesh, in_specs=in_specs, out_specs=out_specs, check_vma=False)

time: 193 us -> 70.5 us (0.37)
  waiting for transfers between devices: 145 us -> 0 us
  Pallas kernels: 0 us -> 64.8 us
  matrix products: 21.4 us -> 0 us
  between operations: 13.1 us -> 0.01 us
  other arithmetic: 9.9 us -> 0 us
  local copies, waits for them, and re-layouts: 1.28 us -> 5.46 us
  blocking collectives: 2.47 us -> 0 us
    reduce_scatter x2 -> x0, waiting for transfers between devices: 83.6 us -> none  [the longest x1 75 us: shards(): branch = lax.psum_scatter(terms, 'gx', scatter_dimension=1, tiled=True)]
    pallas_call x0 -> x1, Pallas kernels: none -> 64.8 us  [fused(): pl.pallas_call(kernel, out_shape=jax.ShapeDtypeStruct((T, wide), BF16), i...]
    all_gather x2 -> x0, waiting for transfers between devices: 60.5 us -> none  [the longest x1 49.5 us: shards(): gathered = lax.all_gather(tokens, 'gx', axis=1, tiled=True)]
    dot_general x2 -> x0, matrix products: 21.4 us -> none  [the longest x1 10.9 us: shards(): jnp.dot(normed, up_weight, preferred_element_type=jnp.float32)]
    convert_element_type x5 -> x0, other arithmetic: 7.75 us -> none  [the longest x1 5.33 us: shards(): jax.nn.gelu(share + bias_up, approximate=False).astype(jnp.bfloat16)]
    reshape x0 -> x3, local copies, waits for them, and re-layouts: none -> 3.84 us  [the longest x1 1.3 us: fused(): ln_gain.reshape(1, -1)]
    psum x1 -> x0, blocking collectives: 2.47 us -> none  [shards(): lax.psum((jnp.sum(all_values, axis=-1), jnp.sum(all_values * all_values,...]
    reduce_sum x1 -> x0, other arithmetic: 2.14 us -> none  [shards(): jnp.sum(all_values, axis=-1)]
  transfers between devices with their start and end apart: 4 -> 0, of which waited for: 4 -> 0; matrix products, arithmetic and copies ran while one was open for 0% -> 0% of each run, Pallas kernels for 0% -> 0%
where the time goes in v1:
time: 70.5 us; the launch traced here: 70.2 us
  Pallas kernels  64.8 us (92%)
  local copies, waits for them, and re-layouts  5.46 us (8%)
    pallas_call x1, Pallas kernels, fused(): pl.pallas_call(kernel, out_shape=jax.ShapeDtypeStruct((T, wide), BF16), i...  64.8 us
    unnamed x1, local copies, waits for them, and re-layouts  1.62 us

profile of v1, /device:TPU:0, one launch (start us, length us, event | category | flops | bytes accessed | tf_op | source)
XLA Modules:
  0.0 70.2 jit_solution(6010699869414592502)
XLA Ops:
  0.0 1.2 %reshape.11.down_bias = bf16[1,384]{1,0:T(2,128)(2,1)} reshape(bf16[384]{0:T(512)(128)(2,1)} %param.11) | data formatting | bytes 1536 | tf_op jit(solution)/shard_map/reshape | solution.py:338
  1.2 1.3 %reshape.9.gain = bf16[1,3072]{1,0:T(2,128)(2,1)} reshape(bf16[3072]{0:T(1024)(128)(2,1)} %param.7) | data formatting | bytes 12288 | tf_op jit(solution)/shard_map/reshape | solution.py:338
  2.5 1.3 %reshape.10.up_bias = bf16[1,3072]{1,0:T(2,128)(2,1)} reshape(bf16[3072]{0:T(1024)(128)(2,1)} %param.9) | data formatting | bytes 12288 | tf_op jit(solution)/shard_map/reshape | solution.py:338
  3.8 64.8 %shard_map.64 = bf16[256,384]{1,0:T(8,128)(2,1)} custom-call(bf16[256,384]{1,0:T(8,128)(2,1)} %tok.1, bf16[1,3072]{1,0:T(2,128)(2,1)} %reshape.9.gain, bf16[1,3072]{1,0:T(2,128)(2,1)} %reshape.10.up_bias, bf16[1,384]{1,0:T(2,128)(2,1)} %reshape.11.down_bias, bf16[3072,3072]{1,0:T(8,128)(2,1)} %wu_hbm.1, bf16[3072,3072]{1,0:T(8,128)(2,1)} %wd_hbm.1), custom_call_target="tpu_custom_call" | custom-call | flops 9663676416 | bytes 37748736 | tf_op jit(solution)/shard_map/pallas_call | solution.py:326
  68.6 1.6 %copy.8 = bf16[256,384]{1,0:T(8,128)(2,1)} copy(bf16[256,384]{1,0:T(8,128)(2,1)} %shard_map.64) | data formatting | bytes 393216

commit v2 on v1

--- a/solution.py
+++ b/solution.py
@@ -45,7 +45,7 @@
 
 
 def kernel(
-    tok, gain, up_bias, down_bias, wu_hbm, wd_hbm, out,
+    tok, gain_in, up_bias_in, down_bias_in, wu_hbm, wd_hbm, out, gain, up_bias, down_bias,
     wu, wd, line, cross, stat, mean_s, scale_s, nrm, acc, p_out, p_in, h_own, h_other,
     y, x_out, x_in, z_out, z_in,
     wu_sem, wd_sem, st_send, st_recv, az_send, az_recv, ax_send, ax_recv,
@@ -54,14 +54,18 @@
     gx, gy = lax.axis_index("gx"), lax.axis_index("gy")
     z, x = gx // 2, gx % 2
     xo, go = 1 - x, 1 - gy
-    zs = (z, z + 1 - 2 * (z % 2), (z + 2) % LINES, LINES - 1 - z)
+    zs = (z, z + 1 - 2 * (z % 2), 2 - z // 2, 3 - 3 * (z // 2))
+    mid = (z + 1) // 2 % 2
+    middle = mid == 1
     rows_all, wide = tok.shape
     R = rows_all // CHUNKS
-    half = acc.shape[1] // 2
+    half = acc.shape[2] // 2
     width = 16 * wide
     to_x = {"gx": z * 2 + xo, "gy": gy}
     to_y = {"gx": gx, "gy": go}
-    to_z = [{"gx": zs[j] * 2 + x, "gy": gy} for j in range(LINES)]
+    to_next = {"gx": zs[1] * 2 + x, "gy": gy}
+    to_middle = {"gx": zs[2] * 2 + x, "gy": gy}
+    to_either = {"gx": (zs[1] + mid * (zs[2] - zs[1])) * 2 + x, "gy": gy}
 
     def rows(c):
         return pl.ds(c * R, R)
@@ -92,46 +96,15 @@
         for a, b in four:
             wd_copy(j, a, b).start()
 
+    gain[...] = gain_in[...].astype(F32).reshape(1, -1)
+    up_bias[...] = up_bias_in[...].astype(F32).reshape(1, -1)
+    down_bias[...] = down_bias_in[...].astype(F32).reshape(1, -1)
+
     me = gx * 2 + gy
     peers = [(me + d) % 16 for d in range(1, 16)]
     barrier = pltpu.get_barrier_semaphore()
     for p in peers:
         pl.semaphore_signal(barrier, inc=1, device_id={"gx": p // 2, "gy": p % 2}, device_id_type=MESH)
-    pl.semaphore_wait(barrier, 15)
-
-    def remote(src, dst, send, recv, where):
-        return pltpu.make_async_remote_copy(
-            src_ref=src, dst_ref=dst, send_sem=send, recv_sem=recv, device_id=where, device_id_type=MESH
-        )
-
-    def gather_z(c, j):
-        return remote(tok.at[rows(c)], line.at[c, j], az_send.at[c, j], az_recv.at[c, j], to_z[j])
-
-    def gather_x(c, j):
-        src = tok.at[rows(c)] if j == 0 else line.at[c, j]
-        return remote(src, cross.at[c, j], ax_send.at[c, j], ax_recv.at[c, j], to_x)
-
-    def pre_copy(c):
-        return remote(p_out.at[c], p_in.at[c], p_sem.at[c, 0], p_sem.at[c, 1], to_y)
-
-    def hid_copy(c):
-        return remote(h_own.at[c], h_other.at[c], h_sem.at[c, 0], h_sem.at[c, 1], to_y)
-
-    def red_x(c, j):
-        return remote(x_out.at[c, j], x_in.at[c, j], rx_send.at[c, j], rx_recv.at[c, j], to_x)
-
-    def red_z(c, j):
-        return remote(z_out.at[c, j], z_in.at[c, j], rz_send.at[c, j], rz_recv.at[c, j], to_z[j])
-
-    def stat_copy(p):
-        return remote(stat.at[me], stat.at[me], st_send.at[p], st_recv.at[me], {"gx": p // 2, "gy": p % 2})
-
-    def stat_arrival(p):
-        return remote(stat.at[p], stat.at[p], st_send.at[p], st_recv.at[p], {"gx": p // 2, "gy": p % 2})
-
-    gather_x(0, 0).start()
-    for j in range(1, LINES):
-        gather_z(0, j).start()
 
     v = tok[...].astype(F32)
     first = jnp.sum(v, axis=1, keepdims=True)
@@ -139,8 +112,70 @@
     lane = lax.broadcasted_iota(jnp.int32, (rows_all, LANES), 1)
     both = jnp.where(lane == 0, first, jnp.where(lane == 1, second, 0.0))
     stat[me] = both.T[0:8, :]
+
+    def remote(src, dst, send, recv, where):
+        return pltpu.make_async_remote_copy(
+            src_ref=src, dst_ref=dst, send_sem=send, recv_sem=recv, device_id=where, device_id_type=MESH
+        )
+
+    def gather_z(c, k):
+        src = tok.at[rows(c)] if k < 2 else line.at[c, k - 1]
+        j = (1, 2, 3, 2, 3)[k]
+        where = to_middle if k in (1, 2) else to_next
+        return remote(src, line.at[c, j], az_send.at[c, k], az_recv.at[c, j], where)
+
+    def line_arrival(c, j):
+        return remote(line.at[c, j], line.at[c, j], az_send.at[c, 0], az_recv.at[c, j], to_next)
+
+    def start_z(c):
+        gather_z(c, 0).start()
+
+        @pl.when(middle)
+        def _():
+            gather_z(c, 1).start()
+
+    def gather_x(c, j):
+        src = tok.at[rows(c)] if j == 0 else line.at[c, j]
+        return remote(src, cross.at[c, j], ax_send.at[c, j], ax_recv.at[c, j], to_x)
+
+    def pre_copy(c):
+        return remote(p_out.at[c], p_in.at[c], p_sem.at[c, 0], p_sem.at[c, 1], to_y)
+
+    def hid_copy(c):
+        return remote(h_own.at[c], h_other.at[c], h_sem.at[c, 0], h_sem.at[c, 1], to_y)
+
+    def red_x(c, j):
+        return remote(x_out.at[c, j], x_in.at[c, j], rx_send.at[c, j], rx_recv.at[c, j], to_x)
+
+    def red_z(c, j):
+        slot = 1 + 3 * mid if j == 1 else j + 2 * mid
+        return remote(
+            z_out.at[c, j], z_in.at[c, slot], rz_send.at[c, j], rz_recv.at[c, slot], to_next if j == 1 else to_either
+        )
+
+    def sum_arrival(c, slot):
+        return remote(z_in.at[c, slot], z_in.at[c, slot], rz_send.at[c, 1], rz_recv.at[c, slot], to_next)
+
+    def stat_copy(p):
+        return remote(stat.at[me], stat.at[me], st_send.at[p], st_recv.at[me], {"gx": p // 2, "gy": p % 2})
+
+    def stat_arrival(p):
+        return remote(stat.at[p], stat.at[p], st_send.at[p], st_recv.at[p], {"gx": p // 2, "gy": p % 2})
+
+    def forward(c, j):
+        line_arrival(c, j).wait_recv()
+        gather_x(c, j).start()
+
+        @pl.when(middle)
+        def _():
+            gather_z(c, j + 1).start()
+
+    pl.semaphore_wait(barrier, 15)
+    start_z(0)
+    gather_x(0, 0).start()
     for p in peers:
         stat_copy(p).start()
+    forward(0, 1)
     for p in peers:
         stat_arrival(p).wait_recv()
     total = stat[0]
@@ -155,17 +190,13 @@
 
     def norm_into(c, j, a, src):
         col = pl.multiple_of((zs[j] * 2 + (x if a == 0 else xo)) * wide, wide)
-        g = gain[:, pl.ds(col, wide)].astype(F32)
+        g = gain[:, pl.ds(col, wide)]
         m = jnp.concatenate([mean_s[rows(c), :]] * (wide // LANES), axis=1)
         s = jnp.concatenate([scale_s[rows(c), :]] * (wide // LANES), axis=1)
         nrm[:, a * wide:(a + 1) * wide] = ((src.astype(F32) - m) * s * g).astype(BF16)
 
     tile = 2 * wide
     tiles = half // tile
-
-    def forward(c, j):
-        gather_z(c, j).wait_recv()
-        gather_x(c, j).start()
 
     def up_step(c, j):
         gather_x(c, j).wait_recv()
@@ -179,12 +210,12 @@
             cols = pl.ds(pl.multiple_of(t * tile, tile), tile)
             part = jnp.dot(nrm[...], wu[j, :, cols], preferred_element_type=F32)
             if j > 0:
-                part = part + acc[:, cols]
+                part = part + acc[c, :, cols]
             if last:
                 out_cols = pl.ds(pl.multiple_of((t - tiles) * tile, tile), tile)
                 p_out[c, :, out_cols] = part.astype(BF16)
             else:
-                acc[:, cols] = part
+                acc[c, :, cols] = part
 
         if j == LINES - 1:
             pl.loop(tiles, 2 * tiles)(lambda t: body(t, True))
@@ -201,7 +232,7 @@
         def _(t):
             cols = pl.ds(pl.multiple_of(t * step, step), step)
             bias_cols = pl.ds(pl.multiple_of(gy * half + t * step, step), step)
-            pre = acc[:, cols] + p_in[c, :, cols].astype(F32) + up_bias[:, bias_cols].astype(F32)
+            pre = acc[c, :, cols] + p_in[c, :, cols].astype(F32) + up_bias[:, bias_cols]
             h_own[c, :, cols] = (0.5 * pre * (1.0 + lax.erf(pre * 0.7071067811865476))).astype(BF16)
 
         hid_copy(c).start()
@@ -218,55 +249,65 @@
 
     def pair_step(c, j):
         red_x(c, j).wait_recv()
-        both = y[c, j] + x_in[c, j].astype(F32)
-        if j == 0:
-            y[c, j] = both
-        else:
-            z_out[c, j] = both.astype(BF16)
+        y[c, j] = y[c, j] + x_in[c, j].astype(F32)
+        if j > 0:
+            slot = (0, 5, 2, 3)[j]
+
+            @pl.when(middle)
+            def _():
+                sum_arrival(c, slot).wait_recv()
+                y[c, j] = y[c, j] + z_in[c, slot].astype(F32)
+
+            z_out[c, j] = y[c, j].astype(BF16)
             red_z(c, j).start()
 
     def finish(c):
-        res = y[c, 0]
-        for j in range(1, LINES):
-            red_z(c, j).wait_recv()
-            res = res + z_in[c, j].astype(F32)
-        res = tok[rows(c), :].astype(F32) + res + down_bias[...].astype(F32)
+        @pl.when(middle)
+        def _():
+            sum_arrival(c, 1).wait_recv()
+            y[c, 0] = y[c, 0] + z_in[c, 1].astype(F32)
+
+        sum_arrival(c, 4).wait_recv()
+        res = y[c, 0] + z_in[c, 4].astype(F32)
+        res = tok[rows(c), :].astype(F32) + res + down_bias[...]
         out[rows(c), :] = res.astype(BF16)
 
-    forward(0, 1)
+    forward(0, 2)
+    start_z(1)
     up_step(0, 0)
-    forward(0, 2)
-    up_step(0, 1)
     forward(0, 3)
     gather_x(1, 0).start()
-    for j in range(1, LINES):
-        gather_z(1, j).start()
+    up_step(0, 1)
+    forward(1, 1)
     up_step(0, 2)
+    forward(1, 2)
     up_step(0, 3)
-    forward(1, 1)
+    forward(1, 3)
+    up_step(1, 0)
     activate(0)
-    forward(1, 2)
-    up_step(1, 0)
+    up_step(1, 1)
     hid_copy(0).wait_recv()
     down_step(0, 3)
-    forward(1, 3)
+    up_step(1, 2)
     down_step(0, 2)
-    up_step(1, 1)
+    up_step(1, 3)
     down_step(0, 1)
+    pair_step(0, 3)
     down_step(0, 0)
-    up_step(1, 2)
-    pair_step(0, 3)
-    up_step(1, 3)
+    activate(1)
     pair_step(0, 2)
-    activate(1)
     pair_step(0, 1)
     pair_step(0, 0)
     hid_copy(1).wait_recv()
-    for j in reversed(range(LINES)):
-        down_step(1, j)
+    down_step(1, 3)
+    down_step(1, 2)
+    down_step(1, 1)
+    pair_step(1, 3)
+    down_step(1, 0)
     finish(0)
-    for j in reversed(range(LINES)):
-        pair_step(1, j)
+    pair_step(1, 2)
+    pair_step(1, 1)
+    pair_step(1, 0)
     finish(1)
 
     for p in peers:
@@ -278,8 +319,13 @@
             gather_x(c, j).wait_send()
             red_x(c, j).wait_send()
             if j > 0:
-                gather_z(c, j).wait_send()
                 red_z(c, j).wait_send()
+        gather_z(c, 0).wait_send()
+
+        @pl.when(middle)
+        def _():
+            for k in range(1, 5):
+                gather_z(c, k).wait_send()
 
 
 def fused(tokens, ln_gain, up_weight, up_bias, down_weight, down_bias):
@@ -290,6 +336,9 @@
     hbm = pl.BlockSpec(memory_space=pl.ANY)
     dma = pltpu.SemaphoreType.DMA
     scratch = [
+        pltpu.VMEM((1, depth), F32),
+        pltpu.VMEM((1, hid), F32),
+        pltpu.VMEM((1, wide), F32),
         pltpu.VMEM((LINES, 2 * wide, hid), BF16),
         pltpu.VMEM((LINES, hid, 2 * wide), BF16),
         pltpu.VMEM((CHUNKS, LINES, R, wide), BF16),
@@ -298,7 +347,7 @@
         pltpu.VMEM((T, LANES), F32),
         pltpu.VMEM((T, LANES), F32),
         pltpu.VMEM((R, 2 * wide), BF16),
-        pltpu.VMEM((R, hid), F32),
+        pltpu.VMEM((CHUNKS, R, hid), F32),
         pltpu.VMEM((CHUNKS, R, half), BF16),
         pltpu.VMEM((CHUNKS, R, half), BF16),
         pltpu.VMEM((CHUNKS, R, half), BF16),
@@ -307,12 +356,12 @@
         pltpu.VMEM((CHUNKS, LINES, R, wide), BF16),
         pltpu.VMEM((CHUNKS, LINES, R, wide), BF16),
         pltpu.VMEM((CHUNKS, LINES, R, wide), BF16),
-        pltpu.VMEM((CHUNKS, LINES, R, wide), BF16),
+        pltpu.VMEM((CHUNKS, 6, R, wide), BF16),
         dma((LINES, 2, 2)),
         dma((LINES, 2, 2)),
         dma((16,)),
         dma((16,)),
-        dma((CHUNKS, LINES)),
+        dma((CHUNKS, 5)),
         dma((CHUNKS, LINES)),
         dma((CHUNKS, LINES)),
         dma((CHUNKS, LINES)),
@@ -321,7 +370,7 @@
         dma((CHUNKS, LINES)),
         dma((CHUNKS, LINES)),
         dma((CHUNKS, LINES)),
-        dma((CHUNKS, LINES)),
+        dma((CHUNKS, 6)),
     ]
     return pl.pallas_call(
         kernel,
@@ -335,7 +384,7 @@
         cost_estimate=pl.CostEstimate(
             flops=4 * T * depth * hid, bytes_accessed=4 * depth * hid, transcendentals=T * half
         ),
-    )(tokens, ln_gain.reshape(1, -1), up_bias.reshape(1, -1), down_bias.reshape(1, -1), up_weight, down_weight)
+    )(tokens, ln_gain, up_bias, down_bias, up_weight, down_weight)
 
 
 def solution(mesh):

time: 70.5 us -> 64.9 us (0.921)
  local copies, waits for them, and re-layouts: 5.46 us -> 1.62 us
  Pallas kernels: 64.8 us -> 63.1 us
    reshape x3 -> x0, local copies, waits for them, and re-layouts: 3.84 us -> none  [the longest x1 1.3 us: fused(): ln_gain.reshape(1, -1)]
    pallas_call x1, Pallas kernels: 64.8 us -> 63.1 us  [fused(): pl.pallas_call(kernel, out_shape=jax.ShapeDtypeStruct((T, wide), BF16), i...]
where the time goes in v2:
time: 64.9 us; the launch traced here: 64.8 us
  Pallas kernels  63.1 us (97%)
  local copies, waits for them, and re-layouts  1.62 us (2%)
    pallas_call x1, Pallas kernels, fused(): pl.pallas_call(kernel, out_shape=jax.ShapeDtypeStruct((T, wide), BF16), i...  63.1 us
    unnamed x1, local copies, waits for them, and re-layouts  1.62 us

profile of v2, /device:TPU:0, one launch (start us, length us, event | category | flops | bytes accessed | tf_op | source)
XLA Modules:
  0.0 64.8 jit_solution(5199759703300841772)
XLA Ops:
  0.0 63.1 %shard_map.64 = bf16[256,384]{1,0:T(8,128)(2,1)} custom-call(bf16[256,384]{1,0:T(8,128)(2,1)} %tok.1, bf16[3072]{0:T(1024)(128)(2,1)} %gain_in.1, bf16[3072]{0:T(1024)(128)(2,1)} %up_bias_in.1, bf16[384]{0:T(512)(128)(2,1)} %down_bias_in.1, bf16[3072,3072]{1,0:T(8,128)(2,1)} %wu_hbm.1, bf16[3072,3072]{1,0:T(8,128)(2,1)} %wd_hbm.1), custom_call_target="tpu_custom_call" | custom-call | flops 9663676416 | bytes 37748736 | tf_op jit(solution)/shard_map/pallas_call | solution.py:375
  63.1 1.6 %copy.8 = bf16[256,384]{1,0:T(8,128)(2,1)} copy(bf16[256,384]{1,0:T(8,128)(2,1)} %shard_map.64) | data formatting | bytes 393216
